TPU v7x, 128 devices: a whole 4x4x4 slice. The times are simulated.
128 devices in a mesh: elem: 8 (over x, core), rve: 16 (over y, z).
Axes of the slice: x: 4, y: 4, z: 4, core: 2. Of those that a mesh axis runs over, the one named last changes fastest.
Arguments:
- displacement: float32 [3, 256], P(None, ('elem', 'rve')), may hold values from -1.75 to 1.75
- connectivity: int32 [8, 256], P(None, ('elem', 'rve')), may hold values from 0 to 255, as said below
- fluctuation: float32 [2048, 6, 4096], P(('elem', 'rve')), may hold values from -1.75 to 1.75
- phases: int32 [2048, 4096], P(('elem', 'rve')), may hold values from 0 to 2
- damage: float32 [2048, 4096], P(('elem', 'rve')), may hold values from 0 to 0.9
- iteration_counts: int32 [2048], P(('elem', 'rve')), may hold values from 1 to 12
- routing: int32 [2048], P(('elem', 'rve')), may hold values from 0 to 15, as said below
- external_force: float32 [3, 256], P(None, ('elem', 'rve')), may hold values from -6 to 6
Outputs:
- residual_force: float32 [3, 256], P(None, ('elem', 'rve'))
- fluctuation_out: float32 [2048, 6, 4096], P(('elem', 'rve'))
- pool_stress: float32 [2048, 6], P(('elem', 'rve'))
Inputs may be any that keep to these rules, and one draw needn't show every extreme that they name: The window is a periodic grid of 4 x 4 x 16 unit elements with renumbered nodes and elements; connectivity[a, e] is the node at corner a = 4 ax + 2 ay + az of element e, offset by ax, ay, az along the three dimensions. `routing`: over the 16 RVEs of one device, a permutation of 0 to 15; value s names pool s // 1 of the same elem index and position s % 1 among that device's RVEs there.
All inputs are finite; a program needn't handle non-finite values.
Results may differ from a plain program's by a relative error of at most 0.0003.
Values sent between devices are 32-bit elements; how exact they have to be, the bound alone decides.
No kernel may reach another device: no remote copies, remote signals or barrier semaphores. Data moves between devices by JAX's collectives and lax.ppermute only.
A program may use at most 64 MiB of HBM per device.

v0:
```python
import math

import jax
import jax.numpy as jnp
from jax import lax
from jax.sharding import PartitionSpec as P

NV = 16


MU_PHASE = (0.1, 0.4, 2.0)
LAM_PHASE = (0.15, 0.6, 1.0)
mu_ref = 1.053
lam_ref = 0.5295
component_pairs = ((0, 0), (1, 1), (2, 2), (1, 2), (0, 2), (0, 1))
component_index = {
    (0, 0): 0,
    (1, 1): 1,
    (2, 2): 2,
    (1, 2): 3,
    (2, 1): 3,
    (0, 2): 4,
    (2, 0): 4,
    (0, 1): 5,
    (1, 0): 5,
}


def shape_gradients():
    lower_coord = 0.5 - 0.5 / math.sqrt(3.0)
    upper_coord = 0.5 + 0.5 / math.sqrt(3.0)
    gradient_table = []
    for corner in range(8):
        corner_bits = (corner >> 2 & 1, corner >> 1 & 1, corner & 1)
        corner_rows = []
        for point_index in range(8):
            point_bits = (point_index >> 2 & 1, point_index >> 1 & 1, point_index & 1)
            coords = [upper_coord if point_flag else lower_coord for point_flag in point_bits]
            factors = [
                coords[axis_index] if corner_bits[axis_index] else 1.0 - coords[axis_index]
                for axis_index in range(3)
            ]
            point_row = []
            for axis_index in range(3):
                entry_value = 1.0 if corner_bits[axis_index] else -1.0
                for other_axis in range(3):
                    if other_axis != axis_index:
                        entry_value = entry_value * factors[other_axis]
                point_row.append(entry_value)
            corner_rows.append(point_row)
        gradient_table.append(corner_rows)
    return gradient_table


def wave_directions():
    line_index = jnp.arange(NV, dtype=jnp.int32)
    wave_line = jnp.where(line_index < (NV + 1) // 2, line_index, line_index - NV).astype(
        jnp.float32
    )
    wave_x, wave_y, wave_z = jnp.meshgrid(wave_line, wave_line, wave_line, indexing="ij")
    length = jnp.sqrt(wave_x**2 + wave_y**2 + wave_z**2)
    safe_length = jnp.where(length > 0, length, 1.0)
    return tuple(
        (
            jnp.where(length > 0, component_wave / safe_length, 0.0)
            for component_wave in (wave_x, wave_y, wave_z)
        )
    )


def moduli(phases, damage):
    softening = (1.0 - damage) ** 2 + 0.05
    shear_modulus = (
        sum(
            (
                jnp.where(phases == phase_level, MU_PHASE[phase_level], 0.0)
                for phase_level in range(3)
            )
        )
        * softening
    )
    lame_modulus = (
        sum(
            (
                jnp.where(phases == phase_level, LAM_PHASE[phase_level], 0.0)
                for phase_level in range(3)
            )
        )
        * softening
    )
    return (shear_modulus, lame_modulus)


def strain_components(deformation):
    return jnp.stack(
        [
            0.5
            * (
                deformation[..., first_axis, second_axis]
                + deformation[..., second_axis, first_axis]
            )
            for first_axis, second_axis in component_pairs
        ],
        axis=-1,
    )


def full_tensor(components):
    rows_list = [
        jnp.stack(
            [components[..., component_index[row_axis, column_axis]] for column_axis in range(3)],
            axis=-1,
        )
        for row_axis in range(3)
    ]
    return jnp.stack(rows_list, axis=-2)


def local_stress(strain, shear_modulus, lame_modulus):
    trace_sum = strain[:, 0] + strain[:, 1] + strain[:, 2]
    pieces = []
    for member in range(6):
        entry_value = 2.0 * shear_modulus * strain[:, member]
        if member < 3:
            entry_value = entry_value + lame_modulus * trace_sum
        pieces.append(entry_value)
    return jnp.stack(pieces, axis=1)


def green_apply(spectra, directions):
    vectors = [
        sum(
            (
                spectra[component_index[row_axis, column_axis]] * directions[column_axis]
                for column_axis in range(3)
            )
        )
        for row_axis in range(3)
    ]
    normal = sum((directions[row_axis] * vectors[row_axis] for row_axis in range(3)))
    volume_term = (lam_ref + mu_ref) / (mu_ref * (lam_ref + 2.0 * mu_ref))
    result = []
    for first_axis, second_axis in component_pairs:
        shear_part = (
            directions[second_axis] * vectors[first_axis]
            + directions[first_axis] * vectors[second_axis]
        ) / (2.0 * mu_ref)
        result.append(
            shear_part - volume_term * directions[first_axis] * directions[second_axis] * normal
        )
    return result


def contract(form, left, right):
    return jnp.einsum(form, left, right, precision=lax.Precision.HIGHEST)


def dft_tables(grid_points):
    line_index = jnp.arange(grid_points, dtype=jnp.int32)
    line_angle = (line_index[:, None] * line_index[None, :] % grid_points).astype(jnp.float32) * (
        2.0 * math.pi / grid_points
    )
    plane_index = jnp.arange(grid_points * grid_points, dtype=jnp.int32)
    plane_y = plane_index // grid_points
    plane_z = plane_index % grid_points
    plane_phase = (
        plane_y[:, None] * plane_y[None, :] + plane_z[:, None] * plane_z[None, :]
    ) % grid_points
    plane_angle = plane_phase.astype(jnp.float32) * (2.0 * math.pi / grid_points)
    return (jnp.cos(line_angle), jnp.sin(line_angle), jnp.cos(plane_angle), jnp.sin(plane_angle))


def solve_block(initial, shear_modulus, lame_modulus, macro_strain, counts, tables, directions):
    cos_line, sin_line, cos_plane, sin_plane = tables
    voxels = initial.shape[2] * initial.shape[3]
    sweep_limit = jnp.max(counts)

    def keep_going(loop_state):
        return loop_state[0] < sweep_limit

    def advance(loop_state):
        step_index, strain = loop_state
        stress_field = local_stress(strain, shear_modulus, lame_modulus)
        plane_real = contract("bcxv,vk->bcxk", stress_field, cos_plane)
        plane_imag = -contract("bcxv,vk->bcxk", stress_field, sin_plane)
        line_real = contract("kx,bcxv->bckv", cos_line, plane_real) + contract(
            "kx,bcxv->bckv", sin_line, plane_imag
        )
        line_imag = contract("kx,bcxv->bckv", cos_line, plane_imag) - contract(
            "kx,bcxv->bckv", sin_line, plane_real
        )
        applied_real = jnp.stack(
            green_apply([line_real[:, member] for member in range(6)], directions), axis=1
        )
        applied_imag = jnp.stack(
            green_apply([line_imag[:, member] for member in range(6)], directions), axis=1
        )
        back_real = contract("kx,bcxv->bckv", cos_line, applied_real) - contract(
            "kx,bcxv->bckv", sin_line, applied_imag
        )
        back_imag = contract("kx,bcxv->bckv", cos_line, applied_imag) + contract(
            "kx,bcxv->bckv", sin_line, applied_real
        )
        update = (
            contract("bcxv,vk->bcxk", back_real, cos_plane)
            - contract("bcxv,vk->bcxk", back_imag, sin_plane)
        ) / voxels
        correction = macro_strain - jnp.mean(strain, axis=(2, 3))
        renewed = strain - update + correction[:, :, None, None]
        active = (step_index < counts)[:, None, None, None]
        return (step_index + 1, jnp.where(active, renewed, strain))

    finished = lax.while_loop(keep_going, advance, (jnp.int32(0), initial))[1]
    stress_mean = jnp.mean(local_stress(finished, shear_modulus, lame_modulus), axis=(2, 3))
    return (finished, stress_mean)


def solve_all(initial, shear_modulus, lame_modulus, macro_strain, counts):
    rve_rows = initial.shape[0]
    plane = NV * NV
    tables = dft_tables(NV)
    directions = tuple(
        (
            jnp.asarray(direction_table.reshape(NV, plane), dtype=jnp.float32)
            for direction_table in wave_directions()
        )
    )
    group_rows = 4
    groups = rve_rows // group_rows

    def solve_group(group_data):
        group_start, group_shear, group_lame, group_macro, group_counts = group_data
        return solve_block(
            group_start, group_shear, group_lame, group_macro, group_counts, tables, directions
        )

    finals, stresses = lax.map(
        solve_group,
        (
            initial.reshape(groups, group_rows, 6, NV, plane),
            shear_modulus.reshape(groups, group_rows, NV, plane),
            lame_modulus.reshape(groups, group_rows, NV, plane),
            macro_strain.reshape(groups, group_rows, 6),
            counts.reshape(groups, group_rows),
        ),
    )
    final_strain = finals.reshape(rve_rows, 6, NV * plane)
    rve_stress = stresses.reshape(rve_rows, 6)
    return (final_strain, rve_stress)


def inverse_slots(routing):
    slot_range = jnp.arange(routing.shape[0], dtype=jnp.int32)
    slot_match = (routing[:, None] == slot_range[None, :]).astype(jnp.int32)
    return jnp.sum(slot_match * slot_range[:, None], axis=0)


def shards(
    displacement,
    connectivity,
    fluctuation,
    phases,
    damage,
    iteration_counts,
    routing,
    external_force,
):
    rve_rows = fluctuation.shape[0]
    element_rows = connectivity.shape[1]
    gradients = jnp.asarray(shape_gradients(), dtype=jnp.float32)
    every_node = lax.all_gather(displacement, ("elem", "rve"), axis=1, tiled=True)
    corner_motion = every_node[:, connectivity]
    deformation = contract("iae,aqj->eqij", corner_motion, gradients)
    macro_strain = strain_components(deformation).reshape(rve_rows, 6)
    shear_modulus, lame_modulus = moduli(phases, damage)
    initial = fluctuation + macro_strain[:, :, None]
    send_order = inverse_slots(routing)
    stacked = jnp.stack((shear_modulus, lame_modulus), axis=1)
    received = (
        lax.all_to_all(initial[send_order], "rve", split_axis=0, concat_axis=0, tiled=True),
        lax.all_to_all(stacked[send_order], "rve", split_axis=0, concat_axis=0, tiled=True),
        lax.all_to_all(macro_strain[send_order], "rve", split_axis=0, concat_axis=0, tiled=True),
        lax.all_to_all(
            iteration_counts[send_order].astype(jnp.float32),
            "rve",
            split_axis=0,
            concat_axis=0,
            tiled=True,
        ),
    )
    pool_strain, pooled = solve_all(
        received[0],
        received[1][:, 0],
        received[1][:, 1],
        received[2],
        received[3].astype(jnp.int32),
    )
    returned = (
        lax.all_to_all(pool_strain, "rve", split_axis=0, concat_axis=0, tiled=True),
        lax.all_to_all(pooled, "rve", split_axis=0, concat_axis=0, tiled=True),
    )
    final_strain = returned[0][routing]
    rve_stress = returned[1][routing]
    fluctuation_out = final_strain - macro_strain[:, :, None]
    stress_tensor = full_tensor(rve_stress).reshape(element_rows, 8, 3, 3)
    corner_force = 0.125 * contract("eqij,aqj->iae", stress_tensor, gradients)
    local_force = (
        jnp.zeros((3, every_node.shape[1]), jnp.float32)
        .at[:, connectivity.reshape(-1)]
        .add(corner_force.reshape(3, -1))
    )
    summed = lax.psum_scatter(local_force, ("elem", "rve"), scatter_dimension=1, tiled=True)
    residual_force = summed - external_force
    return (residual_force, fluctuation_out, pooled)


def solution(mesh):
    return jax.shard_map(
        shards,
        mesh=mesh,
        in_specs=(
            P(None, ("elem", "rve")),
            P(None, ("elem", "rve")),
            P(("elem", "rve"), None, None),
            P(("elem", "rve"), None),
            P(("elem", "rve"), None),
            P(("elem", "rve")),
            P(("elem", "rve")),
            P(None, ("elem", "rve")),
        ),
        out_specs=(
            P(None, ("elem", "rve")),
            P(("elem", "rve"), None, None),
            P(("elem", "rve"), None),
        ),
        check_vma=False,
    )
```

profile of v0, /device:TPU:1, one launch (start us, length us, event | category | flops | bytes accessed | tf_op | source)
XLA Modules:
  0.0 500.7 jit_solution(9424091179525136970)
XLA Ops:
  2.8 8.6 %all-to-all-start.1 = ((f32[16,1,1]{2,1,0:T(1,128)}), f32[16,1,1]{2,1,0:T(1,128)S(1)}, u32[]{:S(2)}, u32[]{:S(2)}) async-start(f32[16,1,1]{2,1,0:T(1,128)} %copy.181), calls=%async_computation.1 | async-start | bytes 16384 | tf_op jit(solution)/shard_map/all_to_all | solution.py:283
  11.4 51.1 %all-gather = f32[128,2,3]{2,1,0:T(2,128)S(1)} all-gather(f32[1,2,3]{2,1,0:T(2,128)} %bitcast.342), channel_id=1, replica_groups=mesh['elem'=8,'rve'=16] {'elem','rve'}, dimensions={0}, use_global_device_ids=true | all-gather | bytes 3096 | tf_op jit(solution)/shard_map/all_gather | solution.py:271
  71.1 3.8 all-to-all-start.2
  74.9 2.4 copy_add_fusion
  77.3 2.0 gather_fusion.1
  79.3 4.8 all-to-all-done.2
  84.1 3.7 all-to-all-start
  91.9 20.9 %all-to-all-done = f32[16,6,4096]{2,1,0:T(8,128)S(1)} async-done(((f32[16,6,4096]{2,1,0:T(8,128)}), f32[16,6,4096]{2,1,0:T(8,128)S(1)}, u32[]{:S(2)}, u32[]{:S(2)}) %all-to-all-start) | async-done | bytes 1572896 | tf_op jit(solution)/shard_map/all_to_all | solution.py:280
  112.8 5.9 %all-to-all-start.3 = ((f32[16,1,6]{2,1,0:T(1,128)}), f32[16,1,6]{2,1,0:T(1,128)S(1)}, u32[]{:S(2)}, u32[]{:S(2)}) async-start(f32[16,1,6]{2,1,0:T(1,128)} %bitcast.54), calls=%async_computation.3 | async-start | bytes 16384 | tf_op jit(solution)/shard_map/all_to_all | solution.py:282
  118.8 2.0 reshape.574
  120.8 4.3 all-to-all-done.3
  125.0 167.0 %while.31 = (s32[]{:T(128)}, f32[4,4,6,16,256]{4,3,2,1,0:T(8,128)}, f32[4,4,6]{2,1,0:T(4,128)}, f32[4,4,6,16,256]{4,3,2,1,0:T(8,128)}, s32[4,4]{1,0:T(4,128)S(1)...) while((s32[]{:T(128)}, f32[4,4,6,16,256]{4,3,2,1,0:T(8,128)}, ...), condition=%wide.region_7.8_spmd.clone.clone.clone, body=%wide.region_1.7_spmd.clone.clone.clone.sunk | while | flops 1363598848 | bytes 23778140 | solution.py:237
  128.6 22.2 %while.32 = (s32[]{:T(128)}, f32[4,6,16,256]{3,2,1,0:T(8,128)S(1)}, s32[]{:T(128)}, s32[4]{0:T(128)S(1)}, f32[16,16,16]{2,1,0:T(8,128)}, /*index=5*/f32[4,16,256...) while((s32[]{:T(128)}, f32[4,6,16,256]{3,2,1,0:T(8,128)S(1)}, ...), condition=%wide.wide.region_5.5_spmd.clone, body=%wide.wide.region_3.4_spmd.clone.sunk | while | flops 1362071552 | bytes 19047108 | solution.py:213
  156.1 22.2 %while.32 = (s32[]{:T(128)}, f32[4,6,16,256]{3,2,1,0:T(8,128)S(1)}, s32[]{:T(128)}, s32[4]{0:T(128)S(1)}, f32[16,16,16]{2,1,0:T(8,128)}, /*index=5*/f32[4,16,256...) while((s32[]{:T(128)}, f32[4,6,16,256]{3,2,1,0:T(8,128)S(1)}, ...), condition=%wide.wide.region_5.5_spmd.clone, body=%wide.wide.region_3.4_spmd.clone.sunk | while | flops 1362071552 | bytes 19047108 | solution.py:213
  183.4 15.0 %while.32 = (s32[]{:T(128)}, f32[4,6,16,256]{3,2,1,0:T(8,128)S(1)}, s32[]{:T(128)}, s32[4]{0:T(128)S(1)}, f32[16,16,16]{2,1,0:T(8,128)}, /*index=5*/f32[4,16,256...) while((s32[]{:T(128)}, f32[4,6,16,256]{3,2,1,0:T(8,128)S(1)}, ...), condition=%wide.wide.region_5.5_spmd.clone, body=%wide.wide.region_3.4_spmd.clone.sunk | while | flops 1362071552 | bytes 19047108 | solution.py:213
  203.7 86.7 %while.32 = (s32[]{:T(128)}, f32[4,6,16,256]{3,2,1,0:T(8,128)S(1)}, s32[]{:T(128)}, s32[4]{0:T(128)S(1)}, f32[16,16,16]{2,1,0:T(8,128)}, /*index=5*/f32[4,16,256...) while((s32[]{:T(128)}, f32[4,6,16,256]{3,2,1,0:T(8,128)S(1)}, ...), condition=%wide.wide.region_5.5_spmd.clone, body=%wide.wide.region_3.4_spmd.clone.sunk | while | flops 1362071552 | bytes 19047108 | solution.py:213
  292.1 109.1 %all-to-all-start.4 = ((f32[16,1,6]{2,1,0:T(1,128)}), f32[16,1,6]{2,1,0:T(1,128)S(1)}, u32[]{:S(2)}, u32[]{:S(2)}) async-start(f32[16,1,6]{2,1,0:T(1,128)} %bitcast.18), calls=%async_computation.4 | async-start | bytes 16384 | tf_op jit(solution)/shard_map/all_to_all | solution.py:300
  401.2 2.9 reshape.575
  404.1 3.5 all-to-all-done.4
  407.6 3.7 all-to-all-start.5
  415.5 78.6 %all-reduce = f32[3,256]{0,1:T(8,128)S(1)} all-reduce(f32[3,256]{0,1:T(8,128)S(1)} %scatter_custom_fusion), channel_id=2, replica_groups=mesh['elem'=8,'rve'=16] {'elem','rve'}, use_global_device_ids=true, to_apply=%region_9.10.clone | all-reduce | flops 768 | bytes 6144
  494.7 2.0 gather_fusion.6
  496.7 1.9 broadcast_subtract_fusion
  498.6 2.1 copy.211
  (766 shorter events, 166.8 us)
Async XLA Ops:
  0.6 0.8 copy-start
  0.6 67.4 %copy-start.4 = (f32[16,4096]{1,0:T(8,128)S(1)}, f32[16,4096]{1,0:T(8,128)}, u32[]{:S(2)}) copy-start(f32[16,4096]{1,0:T(8,128)} %param.17) | copy-start | bytes 786436
  2.8 68.3 %all-to-all-start.1 = ((f32[16,1,1]{2,1,0:T(1,128)}), f32[16,1,1]{2,1,0:T(1,128)S(1)}, u32[]{:S(2)}, u32[]{:S(2)}) async-start(f32[16,1,1]{2,1,0:T(1,128)} %copy.181), calls=%async_computation.1 | async-start | bytes 16384 | tf_op jit(solution)/shard_map/all_to_all | solution.py:283
  71.1 12.9 %all-to-all-start.2 = ((f32[16,2,4096]{2,1,0:T(2,128)}), f32[16,2,4096]{2,1,0:T(2,128)S(1)}, u32[]{:S(2)}, u32[]{:S(2)}) async-start(f32[16,2,4096]{2,1,0:T(2,128)} %gather_fusion.3), calls=%async_computation.2 | async-start | bytes 1048576 | tf_op jit(solution)/shard_map/all_to_all | solution.py:281
  84.1 28.7 %all-to-all-start = ((f32[16,6,4096]{2,1,0:T(8,128)}), f32[16,6,4096]{2,1,0:T(8,128)S(1)}, u32[]{:S(2)}, u32[]{:S(2)}) async-start(f32[16,6,4096]{2,1,0:T(8,128)} %gather_fusion.1), calls=%async_computation | async-start | bytes 4194304 | tf_op jit(solution)/shard_map/all_to_all | solution.py:280
  112.8 12.3 %all-to-all-start.3 = ((f32[16,1,6]{2,1,0:T(1,128)}), f32[16,1,6]{2,1,0:T(1,128)S(1)}, u32[]{:S(2)}, u32[]{:S(2)}) async-start(f32[16,1,6]{2,1,0:T(1,128)} %bitcast.54), calls=%async_computation.3 | async-start | bytes 16384 | tf_op jit(solution)/shard_map/all_to_all | solution.py:282
  127.0 1.6 copy-start.1
  127.0 1.6 copy-start.2
  127.0 1.6 copy-start.3
  154.4 1.6 copy-start.1
  154.5 1.6 copy-start.2
  154.5 1.6 copy-start.3
  181.8 1.6 copy-start.1
  181.8 1.6 copy-start.2
  181.9 1.6 copy-start.3
  202.1 1.6 copy-start.1
  202.1 1.6 copy-start.2
  202.1 1.6 copy-start.3
  292.1 115.5 %all-to-all-start.4 = ((f32[16,1,6]{2,1,0:T(1,128)}), f32[16,1,6]{2,1,0:T(1,128)S(1)}, u32[]{:S(2)}, u32[]{:S(2)}) async-start(f32[16,1,6]{2,1,0:T(1,128)} %bitcast.18), calls=%async_computation.4 | async-start | bytes 16384 | tf_op jit(solution)/shard_map/all_to_all | solution.py:300
  404.0 7.3 %copy-start.6 = (s32[8,2]{0,1:T(2,128)S(1)}, s32[8,2]{0,1:T(2,128)}, u32[]{:S(2)}) copy-start(s32[8,2]{0,1:T(2,128)} %param.14) | copy-start | bytes 196
  404.0 7.4 %copy-start.8 = (s32[16]{0:T(128)S(1)}, s32[16]{0:T(128)}, u32[]{:S(2)}) copy-start(s32[16]{0:T(128)} %param.19) | copy-start | bytes 196
  404.0 10.2 %copy-start.5 = (f32[8,8,3,1]{1,0,2,3:T(8,128)S(1)}, f32[8,8,3,1]{1,0,2,3:T(8,128)}, u32[]{:S(2)}) copy-start(f32[8,8,3,1]{1,0,2,3:T(8,128)} %constant.165) | copy-start | bytes 2308
  404.1 90.0 %copy-start.7 = (f32[3,2]{0,1:T(2,128)S(1)}, f32[3,2]{0,1:T(2,128)}, u32[]{:S(2)}) copy-start(f32[3,2]{0,1:T(2,128)} %param.20) | copy-start | bytes 76
  407.6 87.1 %all-to-all-start.5 = ((f32[16,6,4096]{2,1,0:T(8,128)}), f32[16,6,4096]{2,1,0:T(8,128)S(1)}, u32[]{:S(2)}, u32[]{:S(2)}) async-start(f32[16,6,4096]{2,1,0:T(8,128)} %reshape.575), calls=%async_computation.5 | async-start | bytes 4194304 | tf_op jit(solution)/shard_map/all_to_all | solution.py:299
where the time goes:
time: 502 us; the launch traced here: 501 us
  starting transfers between devices  135 us (27%)
  blocking collectives  130 us (26%)
  matrix products  117 us (23%)
  waiting for transfers between devices  33.4 us (7%)
  other arithmetic  33.1 us (7%)
  local copies, waits for them, and re-layouts  32.4 us (6%)
  loops' own time  19.8 us (4%)
    dot_general x242, matrix products, contract(): return jnp.einsum(form, left, right, precision=lax.Precision.HIGHEST)  117 us
    all_to_all x1, starting transfers between devices, shards(): lax.all_to_all(pooled, 'rve', split_axis=0, concat_axis=0, tiled=True)  109 us
    unnamed x1, blocking collectives  78.6 us
    all_gather x1, blocking collectives, shards(): lax.all_gather(displacement, ('elem', 'rve'), axis=1, tiled=True)  51.1 us
    all_to_all x1, waiting for transfers between devices, shards(): lax.all_to_all(initial[send_order], 'rve', split_axis=0, concat_axis=0, t...  20.9 us
    another operation x4, loops' own time, solve_block(): finished = lax.while_loop(keep_going, advance, (jnp.int32(0), initial))[1]  19.3 us
  transfers between devices with their start and end apart: 6, of which 4 were waited for; matrix products, arithmetic and copies ran while one was open for 5% of the time, Pallas kernels for 0%

commit v1 on v0

v1 whole, which is shorter than its diff:
```python
import math

import jax
import jax.numpy as jnp
import ml_dtypes
import numpy as np
from jax import lax
from jax.experimental import pallas as pl
from jax.experimental.pallas import tpu as pltpu
from jax.sharding import PartitionSpec as P

NV = 16
PLANE = NV * NV
VOX = NV**3
LANES = 128
SLOTS = 8
RVES = 16
ROWS = NV * SLOTS
MU_PHASE = (0.1, 0.4, 2.0)
LAM_PHASE = (0.15, 0.6, 1.0)
mu_ref = 1.053
lam_ref = 0.5295
component_pairs = ((0, 0), (1, 1), (2, 2), (1, 2), (0, 2), (0, 1))
component_index = {tuple(sorted(pair)): c for c, pair in enumerate(component_pairs)}
SQRT2 = math.sqrt(2.0)
MANDEL = (1.0, 1.0, 1.0, SQRT2, SQRT2, SQRT2)
SWAP = (0, 2, 1, 3, 5, 4)
NORMAL_SCALE = (lam_ref + mu_ref) / (lam_ref + 2.0 * mu_ref)
GREEN_SCALE = -2.0 / (mu_ref * VOX)
AXIS_GREEN = {0: 1.0 / (lam_ref + 2.0 * mu_ref), 4: 0.5 / mu_ref, 5: 0.5 / mu_ref}
HIGHEST = lax.Precision.HIGHEST


def shape_gradients():
    lower = 0.5 - 0.5 / math.sqrt(3.0)
    upper = 0.5 + 0.5 / math.sqrt(3.0)
    table = np.zeros((8, 8, 3))
    for corner in range(8):
        bits = (corner >> 2 & 1, corner >> 1 & 1, corner & 1)
        for point in range(8):
            coords = [upper if point >> shift & 1 else lower for shift in (2, 1, 0)]
            factors = [c if b else 1.0 - c for c, b in zip(coords, bits)]
            for axis in range(3):
                entry = 1.0 if bits[axis] else -1.0
                for other in range(3):
                    if other != axis:
                        entry *= factors[other]
                table[corner, point, axis] = entry
    return table


def element_tables():
    gradient = shape_gradients()
    strain = np.zeros((6, RVES, 3, 16))
    force = np.zeros((3, 16, 6, RVES))
    for r in range(RVES):
        e, q = divmod(r, 8)
        for a in range(8):
            j = 2 * a + e
            for c, (k, h) in enumerate(component_pairs):
                strain[c, r, k, j] += 0.5 * gradient[a, q, h]
                strain[c, r, h, j] += 0.5 * gradient[a, q, k]
            for i in range(3):
                for h in range(3):
                    force[i, j, component_index[tuple(sorted((i, h)))], r] += (
                        0.125 * gradient[a, q, h]
                    )
    return strain.reshape(96, 48), force.reshape(48, 96)


def wave(m):
    return m if m < NV // 2 else m - NV


def lane_waves():
    chosen, seen = [], set()
    for ky in range(NV):
        for kz in range(NV):
            partner = (-ky % NV, -kz % NV)
            if (ky, kz) == partner or (ky, kz) in seen:
                continue
            seen.update(((ky, kz), partner))
            chosen.append((ky, kz))
    return chosen


def plane_tables():
    y, z = np.divmod(np.arange(PLANE), NV)
    forward = np.zeros((PLANE, 2 * LANES))
    for lane, (ky, kz) in enumerate(lane_waves()):
        angle = 2.0 * np.pi / NV * ((ky * y + kz * z) % NV)
        forward[:, lane] = np.cos(angle)
        forward[:, LANES + lane] = -np.sin(angle)
    forward[:, 126] = 1.0 - 2.0 * (y % 2)
    forward[:, LANES + 126] = 1.0 - 2.0 * (z % 2)
    forward[:, 127] = 1.0 - 2.0 * ((y + z) % 2)
    forward[:, LANES + 127] = 1.0
    inverse = forward.T.copy()
    inverse[[126, 127, LANES + 126, LANES + 127]] *= 0.5
    return forward, inverse


def split_table(table):
    high = table.astype(ml_dtypes.bfloat16)
    low = (table - high.astype(np.float64)).astype(ml_dtypes.bfloat16)
    return np.concatenate([high, high, low], axis=0)


def green_tables():
    waves = lane_waves() + [(8, 0), (8, 8)]
    out = np.zeros((NV, 12, LANES))
    for kx in range(NV):
        for lane, (ky, kz) in enumerate(waves):
            index = (kx, ky, kz)
            m = np.array([wave(v) for v in index], float)
            back = np.array([wave(-v % NV) for v in index], float)
            length = np.linalg.norm(m)
            if length == 0:
                continue
            n, b = m / length, back / length
            square = n * n
            pair = lambda k, h: 0.5 * (n[k] * n[h] + b[k] * b[h])
            p = [pair(1, 2), pair(0, 2), pair(0, 1)]
            out[kx, 0:3, lane] = square
            out[kx, 3:6, lane] = [v / SQRT2 for v in p]
            for o in range(3):
                k, h = [axis for axis in range(3) if axis != o]
                out[kx, 6 + o, lane] = (
                    0.5 * (square[k] + square[h])
                    - 2.0 * NORMAL_SCALE * square[k] * square[h]
                )
                out[kx, 9 + o, lane] = p[o] * (0.5 - 2.0 * NORMAL_SCALE * square[o])
    return out * GREEN_SCALE


def twiddle(re, im, power, sign):
    power %= 16
    if power == 0:
        return re, im
    if power == 4:
        return (im, -re) if sign < 0 else (-im, re)
    angle = 2.0 * math.pi * power / 16.0
    c, s = math.cos(angle), sign * math.sin(angle)
    if power % 4 == 2:
        root = math.sqrt(0.5)
        cs, ss = math.copysign(1.0, c), math.copysign(1.0, s)
        a = re if cs > 0 else -re
        b = im if cs > 0 else -im
        if cs * ss > 0:
            real, imag = (re - im), (re + im)
        else:
            real, imag = (re + im), (im - re)
        return real * (cs * root), imag * (cs * root)
    return re * c - im * s, re * s + im * c


def dft4(v, sign):
    (ar, ai), (br, bi), (cr, ci), (dr, di) = v
    sr, si, tr, ti = ar + cr, ai + ci, ar - cr, ai - ci
    ur, ui, wr, wi = br + dr, bi + di, br - dr, bi - di
    if sign < 0:
        return [
            (sr + ur, si + ui),
            (tr + wi, ti - wr),
            (sr - ur, si - ui),
            (tr - wi, ti + wr),
        ]
    return [
        (sr + ur, si + ui),
        (tr - wi, ti + wr),
        (sr - ur, si - ui),
        (tr + wi, ti - wr),
    ]


def dft16(values, sign):
    middle = [[None] * 4 for _ in range(4)]
    for first in range(4):
        inner = dft4([values[4 * second + first] for second in range(4)], sign)
        for k in range(4):
            middle[k][first] = twiddle(*inner[k], first * k, sign)
    out = [None] * 16
    for k in range(4):
        outer = dft4(middle[k], sign)
        for high in range(4):
            out[k + 4 * high] = outer[high]
    return out


def green(t, tab):
    double = 2.0 * NORMAL_SCALE / GREEN_SCALE
    xyz = [tab[a] * t[a] for a in range(3)]
    d = (xyz[0] + xyz[1]) + xyz[2]
    o = [tab[3 + a] * t[3 + a] for a in range(3)]
    sums = [o[1] + o[2], o[0] + o[2], o[0] + o[1]]
    s = sums[0] + o[0]
    d2 = d * double
    m = 0.5 * d2 + s * double
    out = [(xyz[a] + sums[a]) - tab[a] * m for a in range(3)]
    for a in range(3):
        k, h = [axis for axis in range(3) if axis != a]
        value = tab[3 + a] * ((t[k] + t[h]) - d2) + tab[6 + a] * t[3 + a]
        value = value + (tab[9 + h] * t[3 + k] + tab[9 + k] * t[3 + h])
        out.append(value)
    return out


def split(value):
    high = value.astype(jnp.bfloat16)
    low = (value - high.astype(jnp.float32)).astype(jnp.bfloat16)
    return high, low


def product(high, low, table_ref):
    left = jnp.concatenate([high, low, high], axis=1)
    return jnp.dot(left, table_ref[...], preferred_element_type=jnp.float32)


def exact(left, right):
    return jnp.dot(left, right, precision=HIGHEST, preferred_element_type=jnp.float32)


def from_scalars(scalars, axis, shape):
    place = lax.broadcasted_iota(jnp.int32, shape, axis)
    out = jnp.full(shape, -1, jnp.int32)
    for index, value in enumerate(scalars):
        out = jnp.where(place == index, value, out)
    return out


def pool_kernel(
    counts,
    routing,
    connectivity,
    elem,
    motion,
    fluctuation,
    phases,
    damage,
    forward,
    inverse,
    tables,
    strain_table,
    force_table,
    fluctuation_out,
    sent,
    order,
    sorted_counts,
    state,
    double_shear,
    lame,
    now_shear,
    now_lame,
    macro,
    now_macro,
    rows,
    parts,
    spectrum,
    table_rows,
    means,
):
    f32 = jnp.float32
    values = [counts[r] for r in range(RVES)]
    for r in range(RVES):
        rank = jnp.int32(0)
        for j in range(RVES):
            if j != r:
                ahead = values[j] >= values[r] if j < r else values[j] > values[r]
                rank = rank + ahead.astype(jnp.int32)
        place = jnp.where(rank < SLOTS, rank, RVES + SLOTS - 1 - rank)
        order[place] = r
        sorted_counts[place] = values[r]
    first = [sorted_counts[s] for s in range(SLOTS)]
    total = [sorted_counts[s] + sorted_counts[SLOTS + s] for s in range(SLOTS)]
    limit = total[0]
    for s in range(1, SLOTS):
        limit = jnp.maximum(limit, total[s])

    nodes = [connectivity[a, e] for a in range(8) for e in range(2)]
    node_rows = from_scalars(nodes, 0, (16, LANES))
    holder = (lax.broadcasted_iota(jnp.int32, (16, LANES), 1) == (node_rows >> 1)).astype(f32)
    corner = exact(holder, motion[...].reshape(LANES, LANES))
    odd = (node_rows & 1) == 1
    moved = [
        jnp.where(
            odd,
            jnp.broadcast_to(corner[:, 3 + i : 4 + i], (16, LANES)),
            jnp.broadcast_to(corner[:, i : i + 1], (16, LANES)),
        )
        for i in range(3)
    ]
    rows[0:96, :] = exact(strain_table[...], jnp.concatenate(moved, axis=0))
    for half in range(2):
        for s in range(SLOTS):
            r = order[half * SLOTS + s]
            for c in range(6):
                macro[half, c, s : s + 1, :] = rows[pl.ds(c * RVES + r, 1), :]

    picked = jnp.concatenate(
        [
            (lax.broadcasted_iota(jnp.int32, (1, RVES), 1) == order[k]).astype(f32)
            for k in range(RVES)
        ],
        axis=0,
    )

    def load(x, carry):
        for side in range(2):
            lanes = pl.ds(pl.multiple_of(x * PLANE + side * LANES, LANES), LANES)
            place = pl.ds(pl.multiple_of(x * SLOTS, SLOTS), SLOTS)
            cut = slice(side * LANES, (side + 1) * LANES)
            phase = exact(picked, phases[:, lanes].astype(f32))
            soft = 1.0 - exact(picked, damage[:, lanes])
            soft = soft * soft + 0.05
            shear = jnp.where(
                phase < 0.5,
                2.0 * MU_PHASE[0],
                jnp.where(phase < 1.5, 2.0 * MU_PHASE[1], 2.0 * MU_PHASE[2]),
            )
            second = jnp.where(
                phase < 0.5,
                LAM_PHASE[0],
                jnp.where(phase < 1.5, LAM_PHASE[1], LAM_PHASE[2]),
            )
            shear, second = shear * soft, second * soft
            for half in range(2):
                double_shear[half, place, cut] = shear[half * SLOTS : (half + 1) * SLOTS]
                lame[half, place, cut] = second[half * SLOTS : (half + 1) * SLOTS]
                block = jnp.stack(
                    [fluctuation[order[half * SLOTS + s], :, lanes] for s in range(SLOTS)], axis=0
                )
                block = jnp.swapaxes(block, 0, 1)
                for c in range(6):
                    state[half, c, place, cut] = (block[c] + macro[half, c]) * MANDEL[c]
        return carry

    lax.fori_loop(0, NV, load, 0)
    now_shear[...] = double_shear[0]
    now_lame[...] = lame[0]
    now_macro[...] = macro[0]
    for kx in range(NV):
        for k in range(12):
            table_rows[kx, k] = jnp.broadcast_to(
                tables[kx * 12 + k : kx * 12 + k + 1, :], (SLOTS, LANES)
            )

    lane = lax.broadcasted_iota(jnp.int32, (SLOTS, LANES), 1)
    first_rows = from_scalars(first, 0, (SLOTS, LANES))
    total_rows = from_scalars(total, 0, (SLOTS, LANES))

    def sweep(step, carry):
        switching = first[0] == step
        ending = total[0] == step
        for s in range(1, SLOTS):
            switching |= first[s] == step
            ending |= total[s] == step

        @pl.when(switching)
        def _():
            mask = first_rows == step
            both = jnp.concatenate([mask, mask], axis=1)

            def exchange(x, inner):
                place = pl.ds(pl.multiple_of(x * SLOTS, SLOTS), SLOTS)
                for c in range(6):
                    old, new = state[0, c, place, :], state[1, c, place, :]
                    state[0, c, place, :] = jnp.where(both, new, old)
                    state[1, c, place, :] = jnp.where(both, old, new)
                now_shear[place, :] = jnp.where(both, double_shear[1, place, :], now_shear[place, :])
                now_lame[place, :] = jnp.where(both, lame[1, place, :], now_lame[place, :])
                return inner

            lax.fori_loop(0, NV, exchange, 0)
            for c in range(6):
                now_macro[c] = jnp.where(mask, macro[1, c], now_macro[c])

        @pl.when(ending)
        def _():
            mask = total_rows == step
            both = jnp.concatenate([mask, mask], axis=1)

            def freeze(x, inner):
                place = pl.ds(pl.multiple_of(x * SLOTS, SLOTS), SLOTS)
                now_shear[place, :] = jnp.where(both, 0.0, now_shear[place, :])
                now_lame[place, :] = jnp.where(both, 0.0, now_lame[place, :])
                return inner

            lax.fori_loop(0, NV, freeze, 0)

        gathered = [None] * 6
        for pair in range(NV // 2):
            place = slice(pair * 16, pair * 16 + 16)
            strain = [state[0, c, place, :] for c in range(6)]
            shear = now_shear[place, :]
            pressure = now_lame[place, :] * ((strain[0] + strain[1]) + strain[2])
            for c in range(6):
                stress = shear * strain[c]
                if c < 3:
                    stress = stress + pressure
                high, low = split(stress)
                parts[c, 0, place, :] = high
                parts[c, 1, place, :] = low
                own = strain[c][:SLOTS] + strain[c][SLOTS:]
                gathered[c] = own if gathered[c] is None else gathered[c] + own
        active = (step < total_rows).astype(f32)
        correction = []
        for c in range(6):
            mean = jnp.sum(gathered[c], axis=1, keepdims=True) * (1.0 / VOX)
            correction.append((now_macro[c] * MANDEL[c] - mean) * active)

        plane = [product(parts[c, 0], parts[c, 1], forward) for c in range(6)]
        for c in range(6):
            line = []
            for x in range(NV):
                place = slice(x * SLOTS, x * SLOTS + SLOTS)
                re, im = plane[c][place, :LANES], plane[c][place, LANES:]
                if SWAP[c] != c:
                    im = jnp.where(lane == 126, plane[SWAP[c]][place, LANES:], im)
                line.append((re, im))
            for kx, (re, im) in enumerate(dft16(line, -1)):
                spectrum[c, kx, 0] = re
                spectrum[c, kx, 1] = im

        axis_values = []
        for c in range(6):
            if c in AXIS_GREEN:
                scale = -2.0 * AXIS_GREEN[c] / PLANE
                offset = 2.0 * correction[c] - (scale / NV) * spectrum[c, 0, 1]
                axis_values.append(
                    [
                        scale * plane[c][x * SLOTS : x * SLOTS + SLOTS, LANES:] + offset
                        for x in range(NV)
                    ]
                )
            else:
                axis_values.append([2.0 * correction[c]] * NV)

        for kx in range(NV):
            tab = [table_rows[kx, k] for k in range(12)]
            for side in range(2):
                out = green([spectrum[c, kx, side] for c in range(6)], tab)
                for c in range(6):
                    spectrum[c, kx, side] = out[c]

        lines = [
            dft16([(spectrum[c, kx, 0], spectrum[c, kx, 1]) for kx in range(NV)], 1)
            for c in range(6)
        ]
        for c in range(6):
            for pair in range(NV // 2):
                re, im = [], []
                for x in (2 * pair, 2 * pair + 1):
                    own = lines[c][x][1]
                    if SWAP[c] != c:
                        own = jnp.where(lane == 126, lines[SWAP[c]][x][1], own)
                    own = jnp.where(lane == 127, axis_values[c][x], own)
                    re.append(lines[c][x][0])
                    im.append(own)
                value = jnp.concatenate(
                    [jnp.concatenate(re, axis=0), jnp.concatenate(im, axis=0)], axis=1
                )
                high, low = split(value)
                parts[c, 0, pair * 16 : pair * 16 + 16, :] = high
                parts[c, 1, pair * 16 : pair * 16 + 16, :] = low
            state[0, c] = state[0, c] + product(parts[c, 0], parts[c, 1], inverse)
        return carry

    lax.fori_loop(0, limit, sweep, 0)

    for half in range(2):
        held = 1 - half

        def gather(x, sums):
            place = pl.ds(pl.multiple_of(x * SLOTS, SLOTS), SLOTS)
            strain = [state[held, c, place, :] for c in range(6)]
            shear = double_shear[half, place, :]
            pressure = lame[half, place, :] * ((strain[0] + strain[1]) + strain[2])
            out = []
            for c in range(6):
                stress = shear * strain[c]
                if c < 3:
                    stress = stress + pressure
                out.append(sums[c] + stress)
            for side in range(2):
                cut = slice(side * LANES, (side + 1) * LANES)
                lanes = pl.ds(pl.multiple_of(x * PLANE + side * LANES, LANES), LANES)
                block = jnp.stack(
                    [
                        strain[c][:, cut] * (1.0 / MANDEL[c]) - macro[half, c]
                        for c in range(6)
                    ],
                    axis=0,
                )
                block = jnp.swapaxes(block, 0, 1)
                for s in range(SLOTS):
                    fluctuation_out[order[half * SLOTS + s], :, lanes] = block[s]
            return tuple(out)

        sums = lax.fori_loop(
            0, NV, gather, tuple(jnp.zeros((SLOTS, PLANE), f32) for _ in range(6))
        )
        for c in range(6):
            mean = jnp.sum(sums[c], axis=1, keepdims=True) * (1.0 / (VOX * MANDEL[c]))
            means[c] = jnp.broadcast_to(mean, (SLOTS, LANES))
        for s in range(SLOTS):
            r = order[half * SLOTS + s]
            for c in range(6):
                rows[pl.ds(c * RVES + r, 1), :] = means[c, s : s + 1, :]

    force = exact(force_table[...], rows[0:96, :])
    column = lax.broadcasted_iota(jnp.int32, (16, LANES), 1)
    right = []
    for low in range(2):
        block = jnp.zeros((16, LANES), f32)
        for i in range(3):
            block = jnp.where(column == 3 * low + i, force[16 * i : 16 * i + 16], block)
        right.append(block)
    block = jnp.zeros((16, LANES), f32)
    for c in range(6):
        block = jnp.where(column == 6 + c, rows[c * RVES : (c + 1) * RVES, :], block)
    right.append(block)
    right.append(jnp.zeros((80, LANES), f32))
    target = [jnp.where((n & 1) == 0, n >> 1, -1) for n in nodes]
    target += [jnp.where((n & 1) == 1, n >> 1, -1) for n in nodes]
    target += [elem[0] * RVES + routing[r] for r in range(RVES)]
    wanted = from_scalars(target, 1, (LANES, LANES))
    taken = (lax.broadcasted_iota(jnp.int32, (LANES, LANES), 0) == wanted).astype(f32)
    sent[...] = exact(taken, jnp.concatenate(right, axis=0)).reshape(LANES, 1, LANES)


def solve(counts, routing, connectivity, elem, motion, fluctuation, phases, damage):
    forward, inverse = (split_table(table) for table in plane_tables())
    strain_table, force_table = element_tables()
    tables = green_tables().reshape(NV * 12, LANES)
    smem = pl.BlockSpec(memory_space=pltpu.SMEM)
    vmem = pl.BlockSpec(memory_space=pltpu.VMEM)
    f32 = jnp.float32
    scratch = [
        pltpu.SMEM((RVES,), jnp.int32),
        pltpu.SMEM((RVES,), jnp.int32),
        pltpu.VMEM((2, 6, ROWS, PLANE), f32),
        pltpu.VMEM((2, ROWS, PLANE), f32),
        pltpu.VMEM((2, ROWS, PLANE), f32),
        pltpu.VMEM((ROWS, PLANE), f32),
        pltpu.VMEM((ROWS, PLANE), f32),
        pltpu.VMEM((2, 6, SLOTS, LANES), f32),
        pltpu.VMEM((6, SLOTS, LANES), f32),
        pltpu.VMEM((96, LANES), f32),
        pltpu.VMEM((6, 2, ROWS, PLANE), jnp.bfloat16),
        pltpu.VMEM((6, NV, 2, SLOTS, LANES), f32),
        pltpu.VMEM((NV, 12, SLOTS, LANES), f32),
        pltpu.VMEM((6, SLOTS, LANES), f32),
    ]
    return pl.pallas_call(
        pool_kernel,
        out_shape=(
            jax.ShapeDtypeStruct((RVES, 6, VOX), f32),
            jax.ShapeDtypeStruct((LANES, 1, LANES), f32),
        ),
        in_specs=[smem] * 4 + [vmem] * 9,
        out_specs=(vmem, vmem),
        scratch_shapes=scratch,
        compiler_params=pltpu.CompilerParams(vmem_limit_bytes=48 * 1024 * 1024),
        name="solve_rves",
    )(
        counts,
        routing,
        connectivity,
        elem,
        motion,
        fluctuation,
        phases,
        damage,
        jnp.asarray(forward),
        jnp.asarray(inverse),
        jnp.asarray(tables, f32),
        jnp.asarray(strain_table, f32),
        jnp.asarray(force_table, f32),
    )


def exchange(rows):
    return lax.all_to_all(rows, ("elem", "rve"), split_axis=0, concat_axis=0, tiled=True)


def shards(
    displacement,
    connectivity,
    fluctuation,
    phases,
    damage,
    iteration_counts,
    routing,
    external_force,
):
    devices = LANES
    own = jnp.pad(displacement.T.reshape(1, 1, 6), ((0, 0), (0, 0), (0, LANES - 6)))
    motion = exchange(jnp.broadcast_to(own, (devices, 1, LANES)))
    elem = lax.axis_index("elem")
    fluctuation_out, sent = solve(
        iteration_counts,
        routing,
        connectivity,
        elem.astype(jnp.int32).reshape(1),
        motion,
        fluctuation,
        phases,
        damage,
    )
    received = exchange(sent)[:, 0, :]
    residual_force = jnp.sum(received[:, :6], axis=0).reshape(2, 3).T - external_force
    pool_stress = lax.dynamic_slice(received, (elem * RVES, 6), (RVES, 6))
    return (residual_force, fluctuation_out, pool_stress)


def solution(mesh):
    both = ("elem", "rve")
    return jax.shard_map(
        shards,
        mesh=mesh,
        in_specs=(
            P(None, both),
            P(None, both),
            P(both, None, None),
            P(both, None),
            P(both, None),
            P(both),
            P(both),
            P(None, both),
        ),
        out_specs=(P(None, both), P(both, None, None), P(both, None)),
        check_vma=False,
    )
```

time: 502 us -> 73.2 us (0.15)
  blocking collectives: 130 us -> 0 us
  matrix products: 117 us -> 0 us
  starting transfers between devices: 135 us -> 35.7 us
  other arithmetic: 33.1 us -> 0.6 us
  waiting for transfers between devices: 33.4 us -> 12.3 us
  local copies, waits for them, and re-layouts: 32.4 us -> 12 us
  loops' own time: 19.8 us -> 0 us
  Pallas kernels: 0 us -> 12.7 us
    dot_general x242 -> x0, matrix products: 117 us -> none  [contract(): return jnp.einsum(form, left, right, precision=lax.Precision.HIGHEST)]
    all_to_all x6 -> x2, starting transfers between devices: 135 us -> 35.7 us  [exchange(): lax.all_to_all(rows, ('elem', 'rve'), split_axis=0, concat_axis=0, tiled=...]
    unnamed x1 -> x0, blocking collectives: 78.6 us -> none
    all_gather x1 -> x0, blocking collectives: 51.1 us -> none  [shards(): lax.all_gather(displacement, ('elem', 'rve'), axis=1, tiled=True)]
    all_to_all x6 -> x2, waiting for transfers between devices: 33.4 us -> 12.3 us  [exchange(): lax.all_to_all(rows, ('elem', 'rve'), split_axis=0, concat_axis=0, tiled=...]
    another operation x5 -> x0, loops' own time: 19.8 us -> none  [the longest x4 19.3 us: solve_block(): finished = lax.while_loop(keep_going, advance, (jnp.int32(0), initial))[1]]
    pallas_call x0 -> x1, Pallas kernels: none -> 12.7 us  [solve(): pl.pallas_call(pool_kernel, out_shape=(jax.ShapeDtypeStruct((RVES, 6, VOX...]
    gather x9 -> x0, local copies, waits for them, and re-layouts: 9.09 us -> none  [the longest x1 2.03 us: shards(): initial[send_order]]
  transfers between devices with their start and end apart: 6 -> 2, of which waited for: 4 -> 2; matrix products, arithmetic and copies ran while one was open for 5% -> 9% of each run, Pallas kernels for 0% -> 0%
where the time goes in v1:
time: 73.2 us; the launch traced here: 74.1 us
  starting transfers between devices  35.7 us (49%)
  Pallas kernels  12.7 us (17%)
  waiting for transfers between devices  12.3 us (17%)
  local copies, waits for them, and re-layouts  12 us (16%)
  between operations  0.76 us (1%)
    all_to_all x2, starting transfers between devices, exchange(): lax.all_to_all(rows, ('elem', 'rve'), split_axis=0, concat_axis=0, tiled=...  35.7 us
    pallas_call x1, Pallas kernels, solve(): pl.pallas_call(pool_kernel, out_shape=(jax.ShapeDtypeStruct((RVES, 6, VOX...  12.7 us
    all_to_all x2, waiting for transfers between devices, exchange(): lax.all_to_all(rows, ('elem', 'rve'), split_axis=0, concat_axis=0, tiled=...  12.3 us
    unnamed x25, local copies, waits for them, and re-layouts  9.67 us
  transfers between devices with their start and end apart: 2, of which 2 were waited for; matrix products, arithmetic and copies ran while one was open for 9% of the time, Pallas kernels for 0%

profile of v1, /device:TPU:1, one launch (start us, length us, event | category | flops | bytes accessed | tf_op | source)
XLA Modules:
  0.0 74.1 jit_solution(12177595556739012064)
XLA Ops:
  0.6 0.0 copy-start.1
  0.6 0.0 copy-start.2
  0.7 0.0 copy-start.6
  0.7 0.0 copy-start.7
  0.7 0.0 copy-start.8
  0.7 0.8 %reshape.19 = f32[1,1,6]{2,1,0:T(1,128)S(1)} reshape(f32[2,3]{1,0:T(2,128)} %bitcast.10) | data formatting | bytes 48 | tf_op jit(solution)/shard_map/reshape | solution.py:597
  1.6 0.7 broadcast_in_dim.8
  2.2 11.5 %all-to-all-start = ((f32[128,1,128]{2,1,0:T(1,128)}), f32[128,1,128]{2,1,0:T(1,128)S(1)}, u32[]{:S(2)}, u32[]{:S(2)}) async-start(f32[128,1,128]{2,1,0:T(1,128)} %broadcast_in_dim.8), calls=%async_computation | async-start | bytes 131072 | tf_op jit(solution)/shard_map/all_to_all | solution.py:583
  13.7 0.8 %copy.16.connectivity = s32[8,2]{1,0:T(8,128)S(1)} copy(s32[8,2]{0,1:T(2,128)} %param.14) | data formatting | bytes 128 | tf_op args[1]
  14.5 2.4 %copy.17.fluctuation = f32[16,6,4096]{2,1,0:T(8,128)S(1)} copy(f32[16,6,4096]{2,0,1:T(8,128)} %param.15) | data formatting | bytes 3145728 | tf_op args[2]
  16.9 6.4 %all-to-all-done.motion = f32[128,1,128]{2,1,0:T(1,128)S(1)} async-done(((f32[128,1,128]{2,1,0:T(1,128)}), f32[128,1,128]{2,1,0:T(1,128)S(1)}, u32[]{:S(2)}, u32[]{:S(2)}) %all-to-all-start) | async-done | bytes 65568 | tf_op jit(solution)/shard_map/all_to_all | solution.py:583
  23.2 0.0 copy-done.1
  23.3 0.0 copy-start.5
  23.3 0.9 %copy-done.5 = f32[192,128]{1,0:T(8,128)S(1)} copy-done((f32[192,128]{1,0:T(8,128)S(1)}, f32[192,128]{1,0:T(8,128)}, u32[]{:S(2)}) %copy-start.5) | copy-done | bytes 98328
  24.2 0.7 copy-done.9
  24.8 12.7 %solve_rves.1 = (f32[16,6,4096]{2,1,0:T(8,128)S(1)}, f32[128,1,128]{2,1,0:T(1,128)}) custom-call(s32[16]{0:T(128)S(1)} %copy-done.8, s32[16]{0:T(128)S(1)} %copy-done.9, s32[8,2]{1,0:T(8,128)S(1)} %copy.16.connectivity, s32[1]{0:T(128)} %bitcast.elem, f32[128,1,128]{2,1,0:T(1,128)S(1)} %all-to-all-done.motion, f32[16,6,4096]{2,1,0:T(8,128)S(1)} %copy.17.fluctuation, ...), custom_call_target="tpu_custom_call" | custom-call | tf_op jit(solution)/shard_map/solve_rves/pallas_call | solution.py:554
  37.5 1.3 %copy-done = f32[16,6,4096]{2,1,0:T(8,128)} copy-done((f32[16,6,4096]{2,1,0:T(8,128)}, f32[16,6,4096]{2,1,0:T(8,128)S(1)}, u32[]{:S(2)}) %copy-start) | copy-done | bytes 1572888
  38.8 24.2 %all-to-all-start.1 = ((f32[128,1,128]{2,1,0:T(1,128)}), f32[128,1,128]{2,1,0:T(1,128)S(1)}, u32[]{:S(2)}, u32[]{:S(2)}) async-start(f32[128,1,128]{2,1,0:T(1,128)} %get-tuple-element.5), calls=%async_computation.1 | async-start | bytes 131072 | tf_op jit(solution)/shard_map/all_to_all | solution.py:583
  63.1 3.6 %copy.19 = f32[16,6,4096]{2,0,1:T(8,128)} copy(f32[16,6,4096]{2,1,0:T(8,128)} %copy-done) | data formatting | bytes 3145728
  66.7 5.9 %all-to-all-done.1 = f32[128,1,128]{2,1,0:T(1,128)S(1)} async-done(((f32[128,1,128]{2,1,0:T(1,128)}), f32[128,1,128]{2,1,0:T(1,128)S(1)}, u32[]{:S(2)}, u32[]{:S(2)}) %all-to-all-start.1) | async-done | bytes 65568 | tf_op jit(solution)/shard_map/all_to_all | solution.py:583
  72.7 0.1 reshape.20
  72.8 0.1 constant_dynamic-slice_fusion
  72.8 0.7 copy.18
  73.5 0.6 bitcast_subtract_fusion
  (14 shorter events, 0.1 us)
Async XLA Ops:
  0.6 22.6 %copy-start.1 = (bf16[768,256]{1,0:T(8,128)(2,1)S(1)}, bf16[768,256]{1,0:T(8,128)(2,1)}, u32[]{:S(2)}) copy-start(bf16[768,256]{1,0:T(8,128)(2,1)} %constant.28.clone.forward) | copy-start | bytes 1179652
  0.6 22.6 %copy-start.2 = (bf16[768,256]{1,0:T(8,128)(2,1)S(1)}, bf16[768,256]{1,0:T(8,128)(2,1)}, u32[]{:S(2)}) copy-start(bf16[768,256]{1,0:T(8,128)(2,1)} %constant.29.clone.inverse) | copy-start | bytes 1179652
  0.7 22.6 %copy-start.6 = (f32[96,48]{1,0:T(8,128)S(1)}, f32[96,48]{1,0:T(8,128)}, u32[]{:S(2)}) copy-start(f32[96,48]{1,0:T(8,128)} %constant.31.clone.strain_table) | copy-start | bytes 55300
  0.7 22.6 %copy-start.7 = (f32[48,96]{1,0:T(8,128)S(1)}, f32[48,96]{1,0:T(8,128)}, u32[]{:S(2)}) copy-start(f32[48,96]{1,0:T(8,128)} %constant.32.clone.force_table) | copy-start | bytes 55300
  0.7 22.6 %copy-start.8 = (s32[16]{0:T(128)S(1)}, s32[16]{0:T(128)}, u32[]{:S(2)}) copy-start(s32[16]{0:T(128)} %counts.1) | copy-start | bytes 196
  0.7 22.6 %copy-start.3 = (s32[16,4096]{1,0:T(8,128)S(1)}, s32[16,4096]{1,0:T(8,128)}, u32[]{:S(2)}) copy-start(s32[16,4096]{1,0:T(8,128)} %phases.1) | copy-start | bytes 786436
  0.7 22.6 %copy-start.4 = (f32[16,4096]{1,0:T(8,128)S(1)}, f32[16,4096]{1,0:T(8,128)}, u32[]{:S(2)}) copy-start(f32[16,4096]{1,0:T(8,128)} %damage.1) | copy-start | bytes 786436
  2.2 21.0 %all-to-all-start = ((f32[128,1,128]{2,1,0:T(1,128)}), f32[128,1,128]{2,1,0:T(1,128)S(1)}, u32[]{:S(2)}, u32[]{:S(2)}) async-start(f32[128,1,128]{2,1,0:T(1,128)} %broadcast_in_dim.8), calls=%async_computation | async-start | bytes 131072 | tf_op jit(solution)/shard_map/all_to_all | solution.py:583
  23.3 0.9 %copy-start.5 = (f32[192,128]{1,0:T(8,128)S(1)}, f32[192,128]{1,0:T(8,128)}, u32[]{:S(2)}) copy-start(f32[192,128]{1,0:T(8,128)} %constant.30.clone.tables) | copy-start | bytes 294916
  24.2 0.7 copy-start.9
  37.5 1.3 %copy-start = (f32[16,6,4096]{2,1,0:T(8,128)}, f32[16,6,4096]{2,1,0:T(8,128)S(1)}, u32[]{:S(2)}) copy-start(f32[16,6,4096]{2,1,0:T(8,128)S(1)} %get-tuple-element.8) | copy-start | bytes 4718596
  38.8 34.7 %copy-start.10 = (f32[3,2]{0,1:T(2,128)S(1)}, f32[3,2]{0,1:T(2,128)}, u32[]{:S(2)}) copy-start(f32[3,2]{0,1:T(2,128)} %param.20) | copy-start | bytes 76
  38.8 33.8 %all-to-all-start.1 = ((f32[128,1,128]{2,1,0:T(1,128)}), f32[128,1,128]{2,1,0:T(1,128)S(1)}, u32[]{:S(2)}, u32[]{:S(2)}) async-start(f32[128,1,128]{2,1,0:T(1,128)} %get-tuple-element.5), calls=%async_computation.1 | async-start | bytes 131072 | tf_op jit(solution)/shard_map/all_to_all | solution.py:583

commit v2 on v1

--- a/solution.py
+++ b/solution.py
@@ -226,6 +226,17 @@
     for index, value in enumerate(scalars):
         out = jnp.where(place == index, value, out)
     return out
+
+
+def column(values):
+    return from_scalars(values, 0, (SLOTS, LANES))
+
+
+def pick(low, high, rows_of):
+    place = rows_of & 7
+    low = jnp.take_along_axis(low, place, axis=0, mode="promise_in_bounds")
+    high = jnp.take_along_axis(high, place, axis=0, mode="promise_in_bounds")
+    return jnp.where(rows_of >= SLOTS, high, low)
 
 
 def pool_kernel(
@@ -258,6 +269,8 @@
     spectrum,
     table_rows,
     means,
+    source,
+    where_is,
 ):
     f32 = jnp.float32
     values = [counts[r] for r in range(RVES)]
@@ -291,47 +304,37 @@
     ]
     rows[0:96, :] = exact(strain_table[...], jnp.concatenate(moved, axis=0))
     for half in range(2):
-        for s in range(SLOTS):
-            r = order[half * SLOTS + s]
-            for c in range(6):
-                macro[half, c, s : s + 1, :] = rows[pl.ds(c * RVES + r, 1), :]
-
-    picked = jnp.concatenate(
-        [
-            (lax.broadcasted_iota(jnp.int32, (1, RVES), 1) == order[k]).astype(f32)
-            for k in range(RVES)
-        ],
-        axis=0,
-    )
+        source[half] = column([order[half * SLOTS + s] for s in range(SLOTS)])
+        for c in range(6):
+            low = rows[c * RVES : c * RVES + SLOTS, :]
+            high = rows[c * RVES + SLOTS : (c + 1) * RVES, :]
+            macro[half, c] = pick(low, high, source[half])
 
     def load(x, carry):
         for side in range(2):
             lanes = pl.ds(pl.multiple_of(x * PLANE + side * LANES, LANES), LANES)
             place = pl.ds(pl.multiple_of(x * SLOTS, SLOTS), SLOTS)
             cut = slice(side * LANES, (side + 1) * LANES)
-            phase = exact(picked, phases[:, lanes].astype(f32))
-            soft = 1.0 - exact(picked, damage[:, lanes])
+            phase = phases[:, lanes]
+            soft = 1.0 - damage[:, lanes]
             soft = soft * soft + 0.05
-            shear = jnp.where(
-                phase < 0.5,
+            shear = soft * jnp.where(
+                phase == 0,
                 2.0 * MU_PHASE[0],
-                jnp.where(phase < 1.5, 2.0 * MU_PHASE[1], 2.0 * MU_PHASE[2]),
+                jnp.where(phase == 1, 2.0 * MU_PHASE[1], 2.0 * MU_PHASE[2]),
             )
-            second = jnp.where(
-                phase < 0.5,
-                LAM_PHASE[0],
-                jnp.where(phase < 1.5, LAM_PHASE[1], LAM_PHASE[2]),
+            second = soft * jnp.where(
+                phase == 0, LAM_PHASE[0], jnp.where(phase == 1, LAM_PHASE[1], LAM_PHASE[2])
             )
-            shear, second = shear * soft, second * soft
             for half in range(2):
-                double_shear[half, place, cut] = shear[half * SLOTS : (half + 1) * SLOTS]
-                lame[half, place, cut] = second[half * SLOTS : (half + 1) * SLOTS]
-                block = jnp.stack(
-                    [fluctuation[order[half * SLOTS + s], :, lanes] for s in range(SLOTS)], axis=0
-                )
-                block = jnp.swapaxes(block, 0, 1)
+                rows_of = source[half]
+                double_shear[half, place, cut] = pick(shear[:SLOTS], shear[SLOTS:], rows_of)
+                lame[half, place, cut] = pick(second[:SLOTS], second[SLOTS:], rows_of)
                 for c in range(6):
-                    state[half, c, place, cut] = (block[c] + macro[half, c]) * MANDEL[c]
+                    block = pick(
+                        fluctuation[c, :SLOTS, lanes], fluctuation[c, SLOTS:, lanes], rows_of
+                    )
+                    state[half, c, place, cut] = (block + macro[half, c]) * MANDEL[c]
         return carry
 
     lax.fori_loop(0, NV, load, 0)
@@ -467,57 +470,61 @@
 
     lax.fori_loop(0, limit, sweep, 0)
 
-    for half in range(2):
-        held = 1 - half
-
-        def gather(x, sums):
-            place = pl.ds(pl.multiple_of(x * SLOTS, SLOTS), SLOTS)
-            strain = [state[held, c, place, :] for c in range(6)]
+    def gather(x, sums):
+        place = pl.ds(pl.multiple_of(x * SLOTS, SLOTS), SLOTS)
+        out = []
+        for half in range(2):
+            strain = [state[1 - half, c, place, :] for c in range(6)]
             shear = double_shear[half, place, :]
             pressure = lame[half, place, :] * ((strain[0] + strain[1]) + strain[2])
-            out = []
             for c in range(6):
                 stress = shear * strain[c]
                 if c < 3:
                     stress = stress + pressure
-                out.append(sums[c] + stress)
-            for side in range(2):
-                cut = slice(side * LANES, (side + 1) * LANES)
-                lanes = pl.ds(pl.multiple_of(x * PLANE + side * LANES, LANES), LANES)
-                block = jnp.stack(
-                    [
-                        strain[c][:, cut] * (1.0 / MANDEL[c]) - macro[half, c]
-                        for c in range(6)
-                    ],
-                    axis=0,
-                )
-                block = jnp.swapaxes(block, 0, 1)
-                for s in range(SLOTS):
-                    fluctuation_out[order[half * SLOTS + s], :, lanes] = block[s]
-            return tuple(out)
-
-        sums = lax.fori_loop(
-            0, NV, gather, tuple(jnp.zeros((SLOTS, PLANE), f32) for _ in range(6))
-        )
+                out.append(sums[6 * half + c] + (stress[:, :LANES] + stress[:, LANES:]))
+                state[1 - half, c, place, :] = strain[c] * (1.0 / MANDEL[c])
+        for side in range(2):
+            cut = slice(side * LANES, (side + 1) * LANES)
+            lanes = pl.ds(pl.multiple_of(x * PLANE + side * LANES, LANES), LANES)
+            for block in range(2):
+                rows_of = source[2 + block]
+                for c in range(6):
+                    ends = [
+                        state[1 - half, c, place, cut] - macro[half, c] for half in range(2)
+                    ]
+                    fluctuation_out[c, block * SLOTS : (block + 1) * SLOTS, lanes] = pick(
+                        *ends, rows_of
+                    )
+        return tuple(out)
+
+    for r in range(RVES):
+        where_is[order[r]] = r
+    for block in range(2):
+        source[2 + block] = column([where_is[block * SLOTS + s] for s in range(SLOTS)])
+    sums = lax.fori_loop(
+        0, NV, gather, tuple(jnp.zeros((SLOTS, LANES), f32) for _ in range(12))
+    )
+    for half in range(2):
         for c in range(6):
-            mean = jnp.sum(sums[c], axis=1, keepdims=True) * (1.0 / (VOX * MANDEL[c]))
-            means[c] = jnp.broadcast_to(mean, (SLOTS, LANES))
-        for s in range(SLOTS):
-            r = order[half * SLOTS + s]
-            for c in range(6):
-                rows[pl.ds(c * RVES + r, 1), :] = means[c, s : s + 1, :]
+            mean = jnp.sum(sums[6 * half + c], axis=1, keepdims=True)
+            mean = mean * (1.0 / (VOX * MANDEL[c]))
+            means[half, c] = jnp.broadcast_to(mean, (SLOTS, LANES))
+    for block in range(2):
+        for c in range(6):
+            base = c * RVES + block * SLOTS
+            rows[base : base + SLOTS, :] = pick(means[0, c], means[1, c], source[2 + block])
 
     force = exact(force_table[...], rows[0:96, :])
-    column = lax.broadcasted_iota(jnp.int32, (16, LANES), 1)
+    lane_of = lax.broadcasted_iota(jnp.int32, (16, LANES), 1)
     right = []
     for low in range(2):
         block = jnp.zeros((16, LANES), f32)
         for i in range(3):
-            block = jnp.where(column == 3 * low + i, force[16 * i : 16 * i + 16], block)
+            block = jnp.where(lane_of == 3 * low + i, force[16 * i : 16 * i + 16], block)
         right.append(block)
     block = jnp.zeros((16, LANES), f32)
     for c in range(6):
-        block = jnp.where(column == 6 + c, rows[c * RVES : (c + 1) * RVES, :], block)
+        block = jnp.where(lane_of == 6 + c, rows[c * RVES : (c + 1) * RVES, :], block)
     right.append(block)
     right.append(jnp.zeros((80, LANES), f32))
     target = [jnp.where((n & 1) == 0, n >> 1, -1) for n in nodes]
@@ -549,12 +556,14 @@
         pltpu.VMEM((6, 2, ROWS, PLANE), jnp.bfloat16),
         pltpu.VMEM((6, NV, 2, SLOTS, LANES), f32),
         pltpu.VMEM((NV, 12, SLOTS, LANES), f32),
-        pltpu.VMEM((6, SLOTS, LANES), f32),
+        pltpu.VMEM((2, 6, SLOTS, LANES), f32),
+        pltpu.VMEM((4, SLOTS, LANES), jnp.int32),
+        pltpu.SMEM((RVES,), jnp.int32),
     ]
     return pl.pallas_call(
         pool_kernel,
         out_shape=(
-            jax.ShapeDtypeStruct((RVES, 6, VOX), f32),
+            jax.ShapeDtypeStruct((6, RVES, VOX), f32),
             jax.ShapeDtypeStruct((LANES, 1, LANES), f32),
         ),
         in_specs=[smem] * 4 + [vmem] * 9,
@@ -603,10 +612,11 @@
         connectivity,
         elem.astype(jnp.int32).reshape(1),
         motion,
-        fluctuation,
+        jnp.transpose(fluctuation, (1, 0, 2)),
         phases,
         damage,
     )
+    fluctuation_out = jnp.transpose(fluctuation_out, (1, 0, 2))
     received = exchange(sent)[:, 0, :]
     residual_force = jnp.sum(received[:, :6], axis=0).reshape(2, 3).T - external_force
     pool_stress = lax.dynamic_slice(received, (elem * RVES, 6), (RVES, 6))

time: 73.2 us -> 77.7 us (1.061); the launches traced: 74.1 us -> 76.4 us
  waiting for transfers between devices: 12.3 us -> 18.3 us
  Pallas kernels: 12.7 us -> 9.78 us
    all_to_all x2, waiting for transfers between devices: 12.3 us -> 18.3 us  [exchange(): lax.all_to_all(rows, ('elem', 'rve'), split_axis=0, concat_axis=0, tiled=...]
    pallas_call x1, Pallas kernels: 12.7 us -> 9.78 us  [solve(): pl.pallas_call(pool_kernel, out_shape=(jax.ShapeDtypeStruct((6, RVES, VOX...]
    unnamed x25 -> x23, local copies, waits for them, and re-layouts: 9.67 us -> 9.79 us
  transfers between devices with their start and end apart: 2 -> 2, of which waited for: 2 -> 2; matrix products, arithmetic and copies ran while one was open for 9% -> 1% of each run, Pallas kernels for 0% -> 0%
where the time goes in v2:
time: 77.7 us; the launch traced here: 76.4 us
  starting transfers between devices  35 us (45%)
  waiting for transfers between devices  18.3 us (24%)
  local copies, waits for them, and re-layouts  12.1 us (16%)
  Pallas kernels  9.78 us (13%)
    all_to_all x2, starting transfers between devices, exchange(): lax.all_to_all(rows, ('elem', 'rve'), split_axis=0, concat_axis=0, tiled=...  35 us
    all_to_all x2, waiting for transfers between devices, exchange(): lax.all_to_all(rows, ('elem', 'rve'), split_axis=0, concat_axis=0, tiled=...  18.3 us
    unnamed x23, local copies, waits for them, and re-layouts  9.79 us
    pallas_call x1, Pallas kernels, solve(): pl.pallas_call(pool_kernel, out_shape=(jax.ShapeDtypeStruct((6, RVES, VOX...  9.78 us
  transfers between devices with their start and end apart: 2, of which 2 were waited for; matrix products, arithmetic and copies ran while one was open for 1% of the time, Pallas kernels for 0%

profile of v2, /device:TPU:1, one launch (start us, length us, event | category | flops | bytes accessed | tf_op | source)
XLA Modules:
  0.0 76.4 jit_solution(16304521193610196953)
XLA Ops:
  0.6 0.8 reshape.19
  1.4 0.7 broadcast_in_dim.8
  2.1 11.5 %all-to-all-start = ((f32[128,1,128]{2,1,0:T(1,128)}), f32[128,1,128]{2,1,0:T(1,128)S(1)}, u32[]{:S(2)}, u32[]{:S(2)}) async-start(f32[128,1,128]{2,1,0:T(1,128)} %broadcast_in_dim.8), calls=%async_computation | async-start | bytes 131072 | tf_op jit(solution)/shard_map/all_to_all | solution.py:592
  13.6 0.8 copy.16.connectivity
  14.3 8.7 %all-to-all-done.motion = f32[128,1,128]{2,1,0:T(1,128)S(1)} async-done(((f32[128,1,128]{2,1,0:T(1,128)}), f32[128,1,128]{2,1,0:T(1,128)S(1)}, u32[]{:S(2)}, u32[]{:S(2)}) %all-to-all-start) | async-done | bytes 65568 | tf_op jit(solution)/shard_map/all_to_all | solution.py:592
  23.1 0.0 copy-start
  23.1 1.4 %copy-done = f32[16,6,4096]{2,0,1:T(8,128)S(1)} copy-done((f32[16,6,4096]{2,0,1:T(8,128)S(1)}, f32[16,6,4096]{2,0,1:T(8,128)}, u32[]{:S(2)}) %copy-start) | copy-done | bytes 1572888
  24.5 1.0 %copy-done.1 = bf16[768,256]{1,0:T(8,128)(2,1)S(1)} copy-done((bf16[768,256]{1,0:T(8,128)(2,1)S(1)}, bf16[768,256]{1,0:T(8,128)(2,1)}, u32[]{:S(2)}) %copy-start.1) | copy-done | bytes 393240
  25.5 1.0 %copy-done.2 = bf16[768,256]{1,0:T(8,128)(2,1)S(1)} copy-done((bf16[768,256]{1,0:T(8,128)(2,1)S(1)}, bf16[768,256]{1,0:T(8,128)(2,1)}, u32[]{:S(2)}) %copy-start.2) | copy-done | bytes 393240
  26.5 0.9 %copy-done.3 = s32[16,4096]{1,0:T(8,128)S(1)} copy-done((s32[16,4096]{1,0:T(8,128)S(1)}, s32[16,4096]{1,0:T(8,128)}, u32[]{:S(2)}) %copy-start.3) | copy-done | bytes 262168
  27.4 0.9 %copy-done.4 = f32[16,4096]{1,0:T(8,128)S(1)} copy-done((f32[16,4096]{1,0:T(8,128)S(1)}, f32[16,4096]{1,0:T(8,128)}, u32[]{:S(2)}) %copy-start.4) | copy-done | bytes 262168
  28.4 0.9 %copy-done.5 = f32[192,128]{1,0:T(8,128)S(1)} copy-done((f32[192,128]{1,0:T(8,128)S(1)}, f32[192,128]{1,0:T(8,128)}, u32[]{:S(2)}) %copy-start.5) | copy-done | bytes 98328
  29.3 0.8 %copy-done.6 = f32[96,48]{1,0:T(8,128)S(1)} copy-done((f32[96,48]{1,0:T(8,128)S(1)}, f32[96,48]{1,0:T(8,128)}, u32[]{:S(2)}) %copy-start.6) | copy-done | bytes 18456
  30.1 0.7 copy-done.7
  30.8 0.7 copy-done.8
  31.5 0.7 copy-done.9
  32.1 9.8 %solve_rves.1 = (f32[6,16,4096]{2,1,0:T(8,128)}, f32[128,1,128]{2,1,0:T(1,128)}) custom-call(s32[16]{0:T(128)S(1)} %copy-done.8, s32[16]{0:T(128)S(1)} %copy-done.9, s32[8,2]{1,0:T(8,128)S(1)} %copy.16.connectivity, s32[1]{0:T(128)} %bitcast.elem, f32[128,1,128]{2,1,0:T(1,128)S(1)} %all-to-all-done.motion, f32[6,16,4096]{2,1,0:T(8,128)S(1)} %bitcast.10, ...), custom_call_target="tpu_custom_call" | custom-call | tf_op jit(solution)/shard_map/solve_rves/pallas_call | solution.py:563
  41.9 23.5 %all-to-all-start.1 = ((f32[128,1,128]{2,1,0:T(1,128)}), f32[128,1,128]{2,1,0:T(1,128)S(1)}, u32[]{:S(2)}, u32[]{:S(2)}) async-start(f32[128,1,128]{2,1,0:T(1,128)} %get-tuple-element.5), calls=%async_computation.1 | async-start | bytes 131072 | tf_op jit(solution)/shard_map/all_to_all | solution.py:592
  65.4 9.6 %all-to-all-done.1 = f32[128,1,128]{2,1,0:T(1,128)S(1)} async-done(((f32[128,1,128]{2,1,0:T(1,128)}), f32[128,1,128]{2,1,0:T(1,128)S(1)}, u32[]{:S(2)}, u32[]{:S(2)}) %all-to-all-start.1) | async-done | bytes 65568 | tf_op jit(solution)/shard_map/all_to_all | solution.py:592
  75.0 0.1 reshape.20
  75.1 0.1 constant_dynamic-slice_fusion
  75.2 0.7 copy.17
  75.9 0.0 copy-done.10
  75.9 0.6 bitcast_subtract_fusion
  (12 shorter events, 0.1 us)
Async XLA Ops:
  2.1 21.0 %all-to-all-start = ((f32[128,1,128]{2,1,0:T(1,128)}), f32[128,1,128]{2,1,0:T(1,128)S(1)}, u32[]{:S(2)}, u32[]{:S(2)}) async-start(f32[128,1,128]{2,1,0:T(1,128)} %broadcast_in_dim.8), calls=%async_computation | async-start | bytes 131072 | tf_op jit(solution)/shard_map/all_to_all | solution.py:592
  23.1 1.4 %copy-start = (f32[16,6,4096]{2,0,1:T(8,128)S(1)}, f32[16,6,4096]{2,0,1:T(8,128)}, u32[]{:S(2)}) copy-start(f32[16,6,4096]{2,0,1:T(8,128)} %param.15) | copy-start | bytes 4718596
  24.5 1.0 %copy-start.1 = (bf16[768,256]{1,0:T(8,128)(2,1)S(1)}, bf16[768,256]{1,0:T(8,128)(2,1)}, u32[]{:S(2)}) copy-start(bf16[768,256]{1,0:T(8,128)(2,1)} %constant.29.clone.inverse) | copy-start | bytes 1179652
  25.5 1.0 %copy-start.2 = (bf16[768,256]{1,0:T(8,128)(2,1)S(1)}, bf16[768,256]{1,0:T(8,128)(2,1)}, u32[]{:S(2)}) copy-start(bf16[768,256]{1,0:T(8,128)(2,1)} %constant.28.clone.forward) | copy-start | bytes 1179652
  26.5 0.9 %copy-start.3 = (s32[16,4096]{1,0:T(8,128)S(1)}, s32[16,4096]{1,0:T(8,128)}, u32[]{:S(2)}) copy-start(s32[16,4096]{1,0:T(8,128)} %phases.1) | copy-start | bytes 786436
  27.4 0.9 %copy-start.4 = (f32[16,4096]{1,0:T(8,128)S(1)}, f32[16,4096]{1,0:T(8,128)}, u32[]{:S(2)}) copy-start(f32[16,4096]{1,0:T(8,128)} %damage.1) | copy-start | bytes 786436
  28.4 0.9 %copy-start.5 = (f32[192,128]{1,0:T(8,128)S(1)}, f32[192,128]{1,0:T(8,128)}, u32[]{:S(2)}) copy-start(f32[192,128]{1,0:T(8,128)} %constant.30.clone.tables) | copy-start | bytes 294916
  29.3 0.8 %copy-start.6 = (f32[96,48]{1,0:T(8,128)S(1)}, f32[96,48]{1,0:T(8,128)}, u32[]{:S(2)}) copy-start(f32[96,48]{1,0:T(8,128)} %constant.31.clone.strain_table) | copy-start | bytes 55300
  30.1 0.7 copy-start.7
  30.8 0.7 copy-start.8
  31.5 0.7 copy-start.9
  32.1 43.8 %copy-start.10 = (f32[3,2]{0,1:T(2,128)S(1)}, f32[3,2]{0,1:T(2,128)}, u32[]{:S(2)}) copy-start(f32[3,2]{0,1:T(2,128)} %param.20) | copy-start | bytes 76
  41.9 33.1 %all-to-all-start.1 = ((f32[128,1,128]{2,1,0:T(1,128)}), f32[128,1,128]{2,1,0:T(1,128)S(1)}, u32[]{:S(2)}, u32[]{:S(2)}) async-start(f32[128,1,128]{2,1,0:T(1,128)} %get-tuple-element.5), calls=%async_computation.1 | async-start | bytes 131072 | tf_op jit(solution)/shard_map/all_to_all | solution.py:592
